TPU v7x, 32 devices: a whole 2x2x4 slice. The times are simulated.
32 devices in a mesh: space: 8 (over z, x), rep: 4 (over y, core).
Axes of the slice: x: 2, y: 2, z: 4, core: 2. Of those that a mesh axis runs over, the one named last changes fastest.
Arguments:
- stem_input: bfloat16 [4, 32, 512, 256], P('rep', 'space'), may hold values from -6 to 6
- stem_preact: bfloat16 [4, 16, 256, 256], P('rep', 'space'), may hold values from -6 to 6
- deep_cotangent: bfloat16 [4, 16, 256, 1024], P('rep', None, 'space'), may hold values from -6 to 6
- tissue_tiles: int32 [4], P('rep'), may hold values from 1 to 64
- conv_weight: bfloat16 [3, 3, 256, 256], replicated, may hold values from -0.125 to 0.125
- expand_weight: bfloat16 [256, 1024], replicated, may hold values from -0.1875 to 0.1875
Outputs:
- grad_input: bfloat16 [4, 32, 512, 256], P('rep', 'space')
- grad_conv: float32 [3, 3, 256, 256], replicated
- grad_expand: float32 [256, 1024], replicated
All inputs are finite; a program needn't handle non-finite values.
Results may differ from a plain program's by a relative error of at most 0.001.
The roundings to bfloat16 on the way count: a program that leaves them out, or rounds other values in their place, can miss the bound.
Values may be sent and summed in bfloat16 or wider, within the bound.
A program may use at most 128 MiB of HBM per device.

v0:
```python
import jax
import jax.numpy as jnp
from jax import lax
from jax.sharding import PartitionSpec as P

TILES = 64


def shifted(x, axis, by):
    length = lax.axis_size(axis)
    pairs = [(i, i + by) for i in range(length) if 0 <= i + by < length]
    return lax.ppermute(x, axis, pairs)


def contract(lhs, rhs):
    return lax.dot_general(
        lhs, rhs, (((0, 1, 2), (0, 1, 2)), ((), ())), preferred_element_type=jnp.float32
    )


def next_column(x):
    return jnp.concatenate([x[:, :, 1:], jnp.zeros_like(x[:, :, :1])], axis=2)


def weight_taps(strip_rows, here, lower):
    samples, rows, cols, channels = strip_rows.shape
    parts = strip_rows.reshape(samples, rows // 2, 2, cols // 2, 2, channels)
    source = {(a, b): parts[:, :, a, :, b] for a in range(2) for b in range(2)}
    taps = []
    for row_tap in range(3):
        grads = lower if row_tap == 0 else here
        for col_tap in range(3):
            grad = next_column(grads) if col_tap == 0 else grads
            taps.append(contract(source[(row_tap + 1) % 2, (col_tap + 1) % 2], grad))
    return jnp.stack(taps, axis=0)


def input_grad(here, lower, conv_weight):
    def term(pieces):
        lhs = jnp.concatenate([grad for grad, _, _ in pieces], axis=3)
        rhs = jnp.concatenate([conv_weight[p, q] for _, p, q in pieces], axis=1)
        out = lax.dot_general(
            lhs, rhs, (((3,), (1,)), ((), ())), preferred_element_type=jnp.float32
        )
        return out.astype(jnp.bfloat16)

    here_next, lower_next = next_column(here), next_column(lower)
    even = [term([(here, 1, 1)]), term([(here, 1, 2), (here_next, 1, 0)])]
    odd = [
        term([(here, 2, 1), (lower, 0, 1)]),
        term([(here, 2, 2), (here_next, 2, 0), (lower, 0, 2), (lower_next, 0, 0)]),
    ]
    both = jnp.stack([jnp.stack(even, axis=3), jnp.stack(odd, axis=3)], axis=2)
    samples, rows, cols, channels = here.shape
    return both.reshape(samples, 2 * rows, 2 * cols, channels)


def body(stem_input, stem_preact, deep_cotangent, tissue_tiles, conv_weight, expand_weight):
    tile_share = tissue_tiles.astype(jnp.float32) / TILES
    weighted = (deep_cotangent.astype(jnp.float32) * tile_share[:, None, None, None]).astype(
        jnp.bfloat16
    )
    hidden_deep = lax.dot_general(
        weighted, expand_weight, (((3,), (1,)), ((), ())), preferred_element_type=jnp.float32
    ).astype(jnp.bfloat16)
    grad_hidden = lax.all_to_all(hidden_deep, "space", split_axis=1, concat_axis=2, tiled=True)
    grad_pre = jnp.where(stem_preact > 0, grad_hidden, jnp.zeros_like(grad_hidden))
    active = jnp.maximum(stem_preact, jnp.zeros_like(stem_preact))
    active_deep = lax.all_to_all(active, "space", split_axis=2, concat_axis=1, tiled=True)
    part_expand = contract(active_deep, weighted)
    below = shifted(grad_pre[:, :1], "space", -1)
    lower = jnp.concatenate([grad_pre[:, 1:], below], axis=1)
    part_conv = weight_taps(stem_input, grad_pre, lower)
    samples_all = stem_input.shape[0] * lax.axis_size("rep")
    rows_all = stem_preact.shape[1] * lax.axis_size("space")
    grad_scale = float(samples_all * rows_all * stem_preact.shape[2]) ** (-0.5)
    channels = conv_weight.shape[2]
    conv_sum, expand_sum = lax.psum((part_conv, part_expand), ("space", "rep"))
    grad_input = input_grad(grad_pre, lower, conv_weight)
    grad_conv = conv_sum.reshape(3, 3, channels, channels) * grad_scale
    return (grad_input, grad_conv, expand_sum * grad_scale)


def solution(mesh):
    return jax.shard_map(
        body,
        mesh=mesh,
        in_specs=(
            P("rep", "space", None, None),
            P("rep", "space", None, None),
            P("rep", None, "space", None),
            P("rep"),
            P(),
            P(),
        ),
        out_specs=(P("rep", "space", None, None), P(), P()),
        check_vma=False,
    )
```

profile of v0, /device:TPU:0, one launch (start us, length us, event | category | flops | bytes accessed | tf_op | source)
XLA Modules:
  0.0 202.5 jit_solution(3775400707885136817)
XLA Ops:
  7.2 0.0 copy-start
  8.0 0.3 copy-done
  8.2 2.5 %fusion.12 = bf16[1,16,32,256]{3,2,0,1:T(8,128)(2,1)} fusion(bf16[1,16,32,1024]{3,2,1,0:T(8,128)(2,1)} %param.8, f32[]{:T(128)} %bitcast, bf16[256,1024]{1,0:T(8,128)(2,1)S(1)} %copy-done), kind=kOutput, calls=%fused_computation.29 | convolution fusion | flops 270139392 | bytes 1835012 | tf_op jit(solution)/shard_map/dot_general | solution.py:63
  10.7 7.3 %all-to-all-start = ((bf16[1,16,32,256]{3,2,0,1:T(8,128)(2,1)}), bf16[1,16,32,256]{3,2,0,1:T(8,128)(2,1)S(1)}, u32[]{:S(2)}, u32[]{:S(2)}) async-start(bf16[1,16,32,256]{3,2,0,1:T(8,128)(2,1)} %fusion.12), calls=%async_computation | async-start | bytes 524288 | tf_op jit(solution)/shard_map/all_to_all | solution.py:66
  17.9 0.4 reshape.100
  18.4 8.5 %all-to-all-done = bf16[1,16,32,256]{3,2,0,1:T(8,128)(2,1)S(1)} async-done(((bf16[1,16,32,256]{3,2,0,1:T(8,128)(2,1)}), bf16[1,16,32,256]{3,2,0,1:T(8,128)(2,1)S(1)}, u32[]{:S(2)}, u32[]{:S(2)}) %all-to-all-start) | async-done | bytes 262176 | tf_op jit(solution)/shard_map/all_to_all | solution.py:66
  26.9 0.1 broadcast_maximum_fusion
  27.0 1.3 collective-permute-start
  28.3 2.6 %fusion.66 = (bf16[1,2,1,256,1,256]{5,4,3,2,1,0:T(2,128)(2,1)}, bf16[1,2,1,256,1,256]{5,4,3,2,1,0:T(2,128)(2,1)}, bf16[1,2,1,256,1,256]{5,4,3,2,1,0:T(2,128)(2,1)}, bf16[1,2,1,256,1,256]{5,4,3,2,1,0:T(2,128)(2,1)}) fusion(bf16[1,2,2,256,2,256]{5,4,3,2,1,0:T(2,128)(2,1)S(1)} %reshape.100), kind=kLoop, calls=%fused_computation.104 | loop fusion | bytes 2097152 | tf_op jit(solution)/shard_map/slice | solution.py:28
  30.8 0.1 slice.71
  30.9 1.0 copy.54
  31.9 4.8 %all-to-all-start.1 = ((bf16[1,2,256,256]{3,1,0,2:T(2,128)(2,1)}), bf16[1,2,256,256]{3,1,0,2:T(2,128)(2,1)}, u32[]{:S(2)}, u32[]{:S(2)}) async-start(bf16[1,2,256,256]{3,1,0,2:T(2,128)(2,1)} %copy.54), calls=%async_computation.1 | async-start | bytes 524288 | tf_op jit(solution)/shard_map/all_to_all | solution.py:69
  36.6 0.0 all-reduce.5.cloned.1.call-start
  36.7 0.0 collective-permute-done
  36.7 0.1 fusion.40
  36.8 0.6 copy-done.10
  37.4 1.4 fusion.11
  38.8 1.4 fusion.10
  40.2 0.0 copy-start.7
  40.2 1.2 fusion.9
  41.5 1.3 fusion.8
  42.8 1.3 fusion.7
  44.1 0.3 fusion.6
  44.4 0.3 fusion.5
  44.7 0.3 fusion.4
  45.0 0.3 fusion.3
  45.3 0.0 copy-start.1
  45.3 0.0 all-to-all-done.1
  45.3 1.2 copy.55
  46.5 2.7 %convolution_bitcast_fusion = f32[256,1024]{1,0:T(8,128)} fusion(bf16[16,32,256]{2,1,0:T(8,128)(2,1)S(1)} %bitcast.192, bf16[1,16,32,1024]{3,2,1,0:T(8,128)(2,1)} %param.8, f32[]{:T(128)} %bitcast), kind=kOutput, calls=%fused_computation.1 | convolution fusion | flops 270008320 | bytes 2359300 | tf_op jit(solution)/shard_map/dot_general | solution.py:16
  49.2 0.0 all-reduce.5.cloned.1.call-update
  49.2 1.2 copy-done.2
  50.5 0.1 slice_bitcast_fusion.7
  50.6 0.3 fusion.1
  50.9 0.3 fusion
  51.2 0.1 maximum_bitcast_fusion.2
  51.3 0.2 copy-done.4
  51.5 0.0 copy-done.11
  51.5 0.3 fusion.2
  51.9 0.5 fusion.13
  52.3 0.1 maximum_bitcast_fusion.5
  52.4 0.1 pad_maximum_fusion
  52.5 1.1 copy.40
  53.6 1.2 reshape.98
  54.8 134.6 %all-reduce.5.cloned.1.call-done = (f32[9,256,256]{1,2,0:T(8,128)}, f32[256,1024]{1,0:T(8,128)}) async-done(((f32[9,256,256]{1,2,0:T(8,128)}, f32[256,1024]{1,0:T(8,128)}), (f32[9,256,256]{1,2,0:T(8,128)}, f32[256,1024]{1,0:T(8,128)})) %all-reduce.5.cloned.1.call-update) | async-done | bytes 3407888 | tf_op jit(solution)/shard_map/psum | solution.py:78
  189.4 1.9 broadcast_multiply_fusion
  191.4 2.0 copy.56
  193.3 2.3 %broadcast_multiply_fusion.1 = f32[256,1024]{1,0:T(8,128)} fusion(f32[256,1024]{1,0:T(8,128)} %get-tuple-element.13), kind=kLoop, calls=%fused_computation.60 | loop fusion | flops 262144 | bytes 2097152 | tf_op jit(solution)/shard_map/mul | solution.py:81
  (20 shorter events, 0.1 us)
Async XLA Ops:
  7.2 1.1 copy-start
  7.2 10.8 %copy-start.5 = (bf16[1,4,512,256]{3,2,1,0:T(8,128)(2,1)S(1)}, bf16[1,4,512,256]{3,2,1,0:T(8,128)(2,1)}, u32[]{:S(2)}) copy-start(bf16[1,4,512,256]{3,2,1,0:T(8,128)(2,1)} %param.6) | copy-start | bytes 3145732
  8.2 18.6 %copy-start.9 = (bf16[1,2,256,256]{3,2,1,0:T(8,128)(2,1)S(1)}, bf16[1,2,256,256]{3,2,1,0:T(8,128)(2,1)}, u32[]{:S(2)}) copy-start(bf16[1,2,256,256]{3,2,1,0:T(8,128)(2,1)} %param.7) | copy-start | bytes 786436
  10.7 16.2 %all-to-all-start = ((bf16[1,16,32,256]{3,2,0,1:T(8,128)(2,1)}), bf16[1,16,32,256]{3,2,0,1:T(8,128)(2,1)S(1)}, u32[]{:S(2)}, u32[]{:S(2)}) async-start(bf16[1,16,32,256]{3,2,0,1:T(8,128)(2,1)} %fusion.12), calls=%async_computation | async-start | bytes 524288 | tf_op jit(solution)/shard_map/all_to_all | solution.py:66
  27.0 9.7 %collective-permute-start = (bf16[1,1,256,256]{3,2,1,0:T(8,128)(2,1)S(1)}, bf16[1,1,256,256]{3,2,1,0:T(8,128)(2,1)S(1)}, u32[]{:S(2)}, u32[]{:S(2)}) collective-permute-start(bf16[1,1,256,256]{3,2,1,0:T(8,128)(2,1)S(1)} %get-tuple-element.28), channel_id=1, source_target_pairs={{4,0},{8,4},{12,8},{16,12},{20,16},{24,20},{28,24},{5,1},{9,5},{13... | collective-permute-start | bytes 393224 | tf_op jit(solution)/shard_map/ppermute | solution.py:12
  31.9 13.4 %all-to-all-start.1 = ((bf16[1,2,256,256]{3,1,0,2:T(2,128)(2,1)}), bf16[1,2,256,256]{3,1,0,2:T(2,128)(2,1)}, u32[]{:S(2)}, u32[]{:S(2)}) async-start(bf16[1,2,256,256]{3,1,0,2:T(2,128)(2,1)} %copy.54), calls=%async_computation.1 | async-start | bytes 524288 | tf_op jit(solution)/shard_map/all_to_all | solution.py:69
  36.6 152.8 %all-reduce.5.cloned.1.call-start = ((), (), s32[]{:S(2)}) async-start(), calls=%async_computation.2 | async-start | bytes 6815744 | tf_op jit(solution)/shard_map/psum | solution.py:78
  36.7 3.5 %copy-start.6 = (bf16[1,2,1,256,1,256]{5,4,3,2,1,0:T(2,128)(2,1)S(1)}, bf16[1,2,1,256,1,256]{5,4,3,2,1,0:T(2,128)(2,1)}, u32[]{:S(2)}) copy-start(bf16[1,2,1,256,1,256]{5,4,3,2,1,0:T(2,128)(2,1)} %get-tuple-element.25) | copy-start | bytes 786436
  36.7 0.7 copy-start.10
  37.4 7.0 %copy-start.3 = (bf16[1,2,255,256]{3,2,1,0:T(8,128)(2,1)}, bf16[1,2,255,256]{3,2,1,0:T(8,128)(2,1)S(1)}, u32[]{:S(2)}) copy-start(bf16[1,2,255,256]{3,2,1,0:T(8,128)(2,1)S(1)} %fusion.40) | copy-start | bytes 783364
  37.4 6.7 %copy-start.8 = (bf16[1,2,1,256,1,256]{5,4,3,2,1,0:T(2,128)(2,1)S(1)}, bf16[1,2,1,256,1,256]{5,4,3,2,1,0:T(2,128)(2,1)}, u32[]{:S(2)}) copy-start(bf16[1,2,1,256,1,256]{5,4,3,2,1,0:T(2,128)(2,1)} %get-tuple-element.23) | copy-start | bytes 786436
  40.2 4.5 %copy-start.7 = (bf16[1,2,1,256,1,256]{5,4,3,2,1,0:T(2,128)(2,1)S(1)}, bf16[1,2,1,256,1,256]{5,4,3,2,1,0:T(2,128)(2,1)}, u32[]{:S(2)}) copy-start(bf16[1,2,1,256,1,256]{5,4,3,2,1,0:T(2,128)(2,1)} %get-tuple-element.24) | copy-start | bytes 786436
  45.3 3.9 %copy-start.1 = (f32[9,256,256]{1,2,0:T(8,128)}, f32[9,256,256]{1,2,0:T(8,128)S(1)}, u32[]{:S(2)}) copy-start(f32[9,256,256]{1,2,0:T(8,128)S(1)} %fusion.3) | copy-start | bytes 7077892
  49.2 1.3 copy-start.2
  50.5 1.0 copy-start.4
  50.6 1.0 copy-start.11
Sparse Core Ops, SparseCore 0:
  49.3 140.0 all-reduce.4
where the time goes:
time: 203 us; the launch traced here: 202 us
  waiting for transfers between devices  143 us (70%)
  between operations  15.1 us (7%)
  matrix products  14.3 us (7%)
  starting transfers between devices  13.3 us (7%)
  local copies, waits for them, and re-layouts  12 us (6%)
  other arithmetic  4.56 us (2%)
    psum x1, waiting for transfers between devices, body(): conv_sum, expand_sum = lax.psum((part_conv, part_expand), ('space', 'rep'))  135 us
    dot_general x10, matrix products, contract(): lax.dot_general(lhs, rhs, (((0, 1, 2), (0, 1, 2)), ((), ())), preferred_e...  10.5 us
    all_to_all x1, waiting for transfers between devices, body(): lax.all_to_all(hidden_deep, 'space', split_axis=1, concat_axis=2, tiled=T...  8.46 us
    all_to_all x1, starting transfers between devices, body(): lax.all_to_all(hidden_deep, 'space', split_axis=1, concat_axis=2, tiled=T...  7.25 us
    all_to_all x1, starting transfers between devices, body(): lax.all_to_all(active, 'space', split_axis=2, concat_axis=1, tiled=True)  4.77 us
    unnamed x25, local copies, waits for them, and re-layouts  4.33 us
  transfers between devices with their start and end apart: 4, of which 2 were waited for; matrix products, arithmetic and copies ran while one was open for 8% of the time, Pallas kernels for 0%

commit v1 on v0

v1 whole, which is shorter than its diff:
```python
import functools

import jax
import jax.numpy as jnp
from jax import lax
from jax.experimental import pallas as pl
from jax.experimental.pallas import tpu as pltpu
from jax.sharding import PartitionSpec as P

TILES = 64
F32, BF16 = jnp.float32, jnp.bfloat16
LEAD = "core"
ORDERS = (("y", "x"), ("x", "y"), ("y", "x"), ("x", "y"))


def dot(lhs, rhs, lhs_dim, rhs_dim):
    return lax.dot_general(
        lhs, rhs, (((lhs_dim,), (rhs_dim,)), ((), ())), preferred_element_type=F32
    )


def layout(n_space, n_rep):
    n_x = 2 if n_space % 2 == 0 else 1
    n_core = 2 if n_rep % 2 == 0 else 1
    return {"z": n_space // n_x, "x": n_x, "y": n_rep // n_core, "core": n_core}


def padded_rows(rows, n_devices):
    unit = 8 * n_devices
    return -(-rows // unit) * unit


def kernel(
    n_space, n_rep, piece_rows, valid_rows,
    share_ref, x_hbm, pre_ref, cot_ref, cw_hbm, ew_ref,
    gi_hbm, gc_hbm, ge_hbm,
    x_ref, cw_ref, weighted, hid_send, hid_recv, act_send, act_recv,
    spread, taps_in, grads, grads_next, below, gi_ref, mixed,
    acc, landing, total,
    load_sem, store_sem, hid_sems, act_sems, below_sems, rs_send, rs_recv, ag_send, ag_recv,
):
    s, r = lax.axis_index("space"), lax.axis_index("rep")
    sizes = layout(n_space, n_rep)
    n_x, n_core = sizes["x"], sizes["core"]
    here = {"z": s // n_x, "x": s % n_x, "y": r // n_core, "core": r % n_core}
    half_rows, width, channels = pre_ref.shape
    band = width // n_space
    block = half_rows * band

    def peer(axis, at):
        if axis == "z":
            return (at * n_x + here["x"], r)
        if axis == "x":
            return (here["z"] * n_x + at, r)
        if axis == "y":
            return (s, at * n_core + here["core"])
        return (s, here["y"] * n_core + at)

    load_x = pltpu.make_async_copy(x_hbm, x_ref, load_sem.at[0])
    load_cw = pltpu.make_async_copy(cw_hbm, cw_ref, load_sem.at[1])
    load_x.start()
    load_cw.start()

    barrier = pltpu.get_barrier_semaphore()
    partners = [((s + d) % n_space, r) for d in range(1, n_space)]
    for axis in ("y", "core"):
        partners += [peer(axis, (here[axis] + d) % sizes[axis]) for d in range(1, sizes[axis])]
    for partner in partners:
        pl.semaphore_signal(
            barrier, inc=1, device_id=partner, device_id_type=pl.DeviceIdType.MESH
        )

    weighted[...] = (cot_ref[...].astype(F32) * share_ref[0]).astype(BF16)
    hidden = dot(weighted[...], ew_ref[...], 1, 1).astype(BF16)
    for j in range(n_space):
        hid_send[j] = hidden[j * block : (j + 1) * block]
    for j in range(n_space):
        for i in range(half_rows):
            rows = pre_ref[i, j * band : (j + 1) * band, :].astype(F32)
            act_send[j, i * band : (i + 1) * band, :] = jnp.maximum(rows, 0.0).astype(BF16)
    pl.semaphore_wait(barrier, len(partners))

    def exchange(source, target, sems):
        copies = []
        for d in range(1, n_space):
            to = (s + d) % n_space
            copies.append(
                pltpu.make_async_remote_copy(
                    src_ref=source.at[to],
                    dst_ref=target.at[s],
                    send_sem=sems.at[0, d],
                    recv_sem=sems.at[1, d],
                    device_id=(to, r),
                    device_id_type=pl.DeviceIdType.MESH,
                )
            )
            copies[-1].start()
        target[s] = source[s]
        return copies

    hid_copies = exchange(hid_send, hid_recv, hid_sems)
    act_copies = exchange(act_send, act_recv, act_sems)

    out_at = lax.broadcasted_iota(jnp.int32, (2 * width, 2 * width), 0)
    in_at = lax.broadcasted_iota(jnp.int32, (2 * width, 2 * width), 1)
    wanted = jnp.where(in_at < width, 2 * in_at, 2 * (in_at - width) + 1)
    spread[...] = jnp.where(out_at == wanted, 1.0, 0.0).astype(BF16)
    load_x.wait()
    for row in range(2 * half_rows):
        split = dot(x_ref[row], spread[...], 0, 0).astype(BF16)
        at = (row // 2) * width
        for parity in range(2):
            taps_in[row % 2, parity, :, at : at + width] = split[
                :, parity * width : (parity + 1) * width
            ]

    for copy in hid_copies:
        copy.wait()

    column = lax.broadcasted_iota(jnp.int32, (width, channels), 0)

    def put_grad(i, value):
        grads[i * width : (i + 1) * width, :] = value.astype(BF16)
        moved = jnp.where(column < width - 1, pltpu.roll(value, width - 1, 0), 0.0)
        grads_next[i * width : (i + 1) * width, :] = moved.astype(BF16)

    for i in range(half_rows):
        arrived = jnp.concatenate(
            [hid_recv[j, i * band : (i + 1) * band, :].astype(F32) for j in range(n_space)], axis=0
        )
        put_grad(i, jnp.where(pre_ref[i].astype(F32) > 0, arrived, 0.0))
    below_copy = pltpu.make_async_remote_copy(
        src_ref=grads.at[0:width],
        dst_ref=below,
        send_sem=below_sems.at[0],
        recv_sem=below_sems.at[1],
        device_id=((s + n_space - 1) % n_space, r),
        device_id_type=pl.DeviceIdType.MESH,
    )

    @pl.when(s > 0)
    def _():
        below_copy.start()

    starts = [sum(piece_rows[:k]) for k in range(len(piece_rows))]
    span = half_rows * width

    def conv_piece(k, row_tap):
        first = width if row_tap == 0 else 0
        for col_tap in range(3):
            grad = grads_next if col_tap == 0 else grads
            at = starts[k] + col_tap * channels
            acc[at : at + channels, :] = dot(
                taps_in[(row_tap + 1) % 2, (col_tap + 1) % 2], grad[first : first + span, :], 1, 0
            )

    def piece(k):
        if piece_rows[k] > valid_rows[k]:
            acc[starts[k] + valid_rows[k] : starts[k] + piece_rows[k], :] = jnp.zeros(
                (piece_rows[k] - valid_rows[k], acc.shape[1]), F32
            )
        base, length = starts[k], piece_rows[k]
        slot, sem = starts[k], 0
        levels = []
        for axis in (LEAD,) + ORDERS[k] + ("z",):
            n, at = sizes[axis], here[axis]
            if n == 1:
                continue
            sub = length // n
            copies, slots = [], []
            for d in range(1, n):
                to = (at + d) % n
                copies.append(
                    pltpu.make_async_remote_copy(
                        src_ref=acc.at[pl.ds(pl.multiple_of(base + to * sub, 8), sub)],
                        dst_ref=landing.at[pl.ds(slot, sub)],
                        send_sem=rs_send.at[k, sem],
                        recv_sem=rs_recv.at[k, sem],
                        device_id=peer(axis, to),
                        device_id_type=pl.DeviceIdType.MESH,
                    )
                )
                copies[-1].start()
                slots.append(slot)
                slot += sub
                sem += 1
            yield
            for copy in copies:
                copy.wait()
            base = base + at * sub
            own = pl.ds(pl.multiple_of(base, 8), sub)
            value = acc[own, :]
            for place in slots:
                value = value + landing[place : place + sub, :]
            acc[own, :] = value
            length = sub
            levels.append((axis, n, at, base, sub))
        total[own, :] = value
        sem = 0
        for axis, n, at, base, sub in reversed(levels):
            copies = []
            mine = total.at[pl.ds(pl.multiple_of(base, 8), sub)]
            for d in range(1, n):
                copies.append(
                    pltpu.make_async_remote_copy(
                        src_ref=mine,
                        dst_ref=mine,
                        send_sem=ag_send.at[k, sem],
                        recv_sem=ag_recv.at[k, sem],
                        device_id=peer(axis, (at + d) % n),
                        device_id_type=pl.DeviceIdType.MESH,
                    )
                )
                copies[-1].start()
                sem += 1
            yield
            for copy in copies:
                copy.wait()

    pieces = [piece(k) for k in range(4)]
    conv_piece(0, 1)
    next(pieces[0])
    conv_piece(1, 2)
    next(pieces[1])

    @pl.when(s < n_space - 1)
    def _():
        below_copy.wait_recv()

    last = jnp.where(s < n_space - 1, 1.0, 0.0)
    lower = below[...].astype(F32)
    put_grad(half_rows, jnp.where(last > 0.5, lower, 0.0))
    next(pieces[0])
    conv_piece(2, 0)
    next(pieces[2])
    next(pieces[1])
    for copy in act_copies:
        copy.wait()
    active = act_recv[...].astype(F32).reshape(n_space * block, channels).astype(BF16)
    deep = weighted.shape[1]
    for k in range(deep // channels):
        at = starts[3] + k * channels
        acc[at : at + channels, :] = dot(
            active, weighted[:, k * channels : (k + 1) * channels], 0, 0
        )
    next(pieces[3])
    next(pieces[2])
    next(pieces[3])

    load_cw.wait()

    def term(first, row_tap, col_tap):
        grad = grads_next if col_tap == 0 else grads
        return dot(grad[first : first + span, :], cw_ref[row_tap, col_tap], 1, 1)

    stores = []
    for row_parity in range(2):
        pairs = [(0, 1)] if row_parity == 0 else [(0, 2), (width, 0)]
        for parity in range(2):
            cols = (1,) if parity == 0 else (2, 0)
            terms = [term(first, p, q) for first, p in pairs for q in cols]
            mixed[parity] = functools.reduce(jnp.add, terms).astype(BF16)
        for i in range(half_rows):
            both = jnp.concatenate(
                [mixed[parity, i * width : (i + 1) * width, :] for parity in range(2)], axis=0
            )
            row = 2 * i + row_parity
            gi_ref[row] = dot(spread[...], both, 1, 0).astype(BF16)
            stores.append(
                pltpu.make_async_copy(gi_ref.at[row], gi_hbm.at[row], store_sem.at[row])
            )
            stores[-1].start()

    slot = 2 * half_rows
    waiting = list(range(4))
    while waiting:
        for k in list(waiting):
            if next(pieces[k], "end") != "end":
                continue
            waiting.remove(k)
            if k < 3:
                rows = total.at[pl.ds(starts[k], valid_rows[k])]
                outs = [(rows, gc_hbm.at[(1, 2, 0)[k]])]
            else:
                outs = [
                    (
                        total.at[pl.ds(starts[k] + m * channels, channels)],
                        ge_hbm.at[:, pl.ds(m * channels, channels)],
                    )
                    for m in range(deep // channels)
                ]
            for source, target in outs:
                stores.append(pltpu.make_async_copy(source, target, store_sem.at[slot]))
                stores[-1].start()
                slot += 1

    @pl.when(s > 0)
    def _():
        below_copy.wait_send()

    for store in stores:
        store.wait()


def body(n_space, n_rep, stem_input, stem_preact, deep_cotangent, tissue_tiles, conv_weight, expand_weight):
    share = tissue_tiles.astype(F32) / TILES
    _, in_rows, cols, channels = stem_input.shape
    _, half_rows, width, _ = stem_preact.shape
    _, deep_rows, band, deep = deep_cotangent.shape
    devices = n_space * n_rep
    block = half_rows * band
    valid_rows = [3 * channels] * 3 + [deep]
    piece_rows = [padded_rows(rows, devices) for rows in valid_rows]
    all_rows = sum(piece_rows)
    sizes = layout(n_space, n_rep)
    copies = sum(n - 1 for n in sizes.values())
    vmem = pl.BlockSpec(memory_space=pltpu.VMEM)
    anywhere = pl.BlockSpec(memory_space=pl.ANY)
    dma = pltpu.SemaphoreType.DMA
    grad_input, conv_sum, expand_sum = pl.pallas_call(
        functools.partial(kernel, n_space, n_rep, piece_rows, valid_rows),
        out_shape=(
            jax.ShapeDtypeStruct((in_rows, cols, channels), BF16),
            jax.ShapeDtypeStruct((3, 3 * channels, channels), F32),
            jax.ShapeDtypeStruct((channels, deep), F32),
        ),
        in_specs=[
            pl.BlockSpec(memory_space=pltpu.SMEM),
            anywhere,
            vmem,
            vmem,
            anywhere,
            vmem,
        ],
        out_specs=(anywhere, anywhere, anywhere),
        scratch_shapes=[
            pltpu.VMEM((in_rows, cols, channels), BF16),
            pltpu.VMEM(conv_weight.shape, BF16),
            pltpu.VMEM((deep_rows * band, deep), BF16),
            pltpu.VMEM((n_space, block, channels), BF16),
            pltpu.VMEM((n_space, block, channels), BF16),
            pltpu.VMEM((n_space, block, channels), BF16),
            pltpu.VMEM((n_space, block, channels), BF16),
            pltpu.VMEM((cols, cols), BF16),
            pltpu.VMEM((2, 2, channels, half_rows * width), BF16),
            pltpu.VMEM(((half_rows + 1) * width, channels), BF16),
            pltpu.VMEM(((half_rows + 1) * width, channels), BF16),
            pltpu.VMEM((width, channels), BF16),
            pltpu.VMEM((in_rows, cols, channels), BF16),
            pltpu.VMEM((2, half_rows * width, channels), BF16),
            pltpu.VMEM((all_rows, channels), F32),
            pltpu.VMEM((all_rows, channels), F32),
            pltpu.VMEM((all_rows, channels), F32),
            dma((2,)),
            dma((in_rows + 3 + deep // channels,)),
            dma((2, n_space)),
            dma((2, n_space)),
            dma((2,)),
            dma((4, copies)),
            dma((4, copies)),
            dma((4, copies)),
            dma((4, copies)),
        ],
        compiler_params=pltpu.CompilerParams(
            collective_id=0, has_side_effects=True, vmem_limit_bytes=56 * 1024 * 1024
        ),
    )(
        share,
        stem_input[0],
        stem_preact[0],
        deep_cotangent.reshape(deep_rows * band, deep),
        conv_weight,
        expand_weight,
    )
    grad_scale = float(n_rep * half_rows * n_space * width) ** (-0.5)
    grad_conv = conv_sum.reshape(3, 3, channels, channels) * grad_scale
    return (grad_input[None], grad_conv, expand_sum * grad_scale)


def solution(mesh):
    return jax.shard_map(
        functools.partial(body, mesh.shape["space"], mesh.shape["rep"]),
        mesh=mesh,
        in_specs=(
            P("rep", "space", None, None),
            P("rep", "space", None, None),
            P("rep", None, "space", None),
            P("rep"),
            P(),
            P(),
        ),
        out_specs=(P("rep", "space", None, None), P(), P()),
        check_vma=False,
    )
```

time: 203 us -> 79.7 us (0.39)
  the two profiles are of different devices: /device:TPU:0 before, /device:TPU:25 now
where the time goes in v1:
time: 79.7 us; the launch traced here: 79.5 us
  Pallas kernels  71.6 us (90%)
  other arithmetic  5.67 us (7%)
  between operations  1.29 us (2%)
  local copies, waits for them, and re-layouts  0.97 us (1%)
    pallas_call x1, Pallas kernels, body(): pl.pallas_call(functools.partial(kernel, n_space, n_rep, piece_rows, vali...  71.6 us
    mul x1, other arithmetic, body(): grad_conv = conv_sum.reshape(3, 3, channels, channels) * grad_scale  3.36 us
    mul x1, other arithmetic, body(): return (grad_input[None], grad_conv, expand_sum * grad_scale)  2.31 us

profile of v1, /device:TPU:25, one launch (start us, length us, event | category | flops | bytes accessed | tf_op | source)
XLA Modules:
  0.0 79.5 jit_solution(3649541027720549297)
XLA Ops:
  1.3 71.6 %shard_map.85 = (bf16[4,512,256]{2,1,0:T(8,128)(2,1)}, f32[3,768,256]{2,1,0:T(8,128)}, f32[256,1024]{1,0:T(8,128)}) custom-call(f32[1]{0:T(128)S(6)} %div.3.share_ref, bf16[4,512,256]{2,1,0:T(8,128)(2,1)} %bitcast.7, bf16[2,256,256]{2,1,0:T(8,128)(2,1)} %bitcast.9, bf16[512,1024]{1,0:T(8,128)(2,1)} %bitcast.8, bf16[3,3,256,256]{3,2,1,0:T(8,128)(2,1)} %cw_hbm.1, ...), custom_call_target="tpu_custom_call" | custom-call | tf_op jit(solution)/shard_map/pallas_call | solution.py:320
  72.8 2.3 %broadcast_multiply_fusion.1 = f32[256,1024]{1,0:T(8,128)} fusion(f32[256,1024]{1,0:T(8,128)} %get-tuple-element.8), kind=kLoop, calls=%fused_computation.1 | loop fusion | flops 262144 | bytes 2097152 | tf_op jit(solution)/shard_map/mul | solution.py:377
  75.2 0.0 copy-start
  75.2 3.4 %broadcast_multiply_fusion = f32[3,768,256]{2,1,0:T(8,128)} fusion(f32[3,768,256]{2,1,0:T(8,128)} %get-tuple-element.7), kind=kLoop, calls=%fused_computation | loop fusion | flops 589824 | bytes 4718592 | tf_op jit(solution)/shard_map/mul | solution.py:376
  78.5 0.0 copy-done
  78.5 1.0 %copy.11 = bf16[1,4,512,256]{3,2,1,0:T(8,128)(2,1)} copy(bf16[1,4,512,256]{3,2,1,0:T(8,128)(2,1)S(1)} %bitcast.6) | data formatting | bytes 2097152
Async XLA Ops:
  75.2 3.4 %copy-start = (bf16[4,512,256]{2,1,0:T(8,128)(2,1)S(1)}, bf16[4,512,256]{2,1,0:T(8,128)(2,1)}, u32[]{:S(2)}) copy-start(bf16[4,512,256]{2,1,0:T(8,128)(2,1)} %get-tuple-element.6) | copy-start | bytes 3145732

commit v2 on v1

--- a/solution.py
+++ b/solution.py
@@ -1,4 +1,5 @@
 import functools
+import heapq
 
 import jax
 import jax.numpy as jnp
@@ -8,9 +9,10 @@
 from jax.sharding import PartitionSpec as P
 
 TILES = 64
+VMEM_LIMIT = 32 * 1024 * 1024
 F32, BF16 = jnp.float32, jnp.bfloat16
-LEAD = "core"
-ORDERS = (("y", "x"), ("x", "y"), ("y", "x"), ("x", "y"))
+ORDERS = ("xyz", "yxz", "xzy", "yxz", "xyz", "yzx")
+UNITS = tuple((p, q) for p in (1, 2, 0) for q in range(3))
 
 
 def dot(lhs, rhs, lhs_dim, rhs_dim):
@@ -31,10 +33,10 @@
 
 
 def kernel(
-    n_space, n_rep, piece_rows, valid_rows,
-    share_ref, x_hbm, pre_ref, cot_ref, cw_hbm, ew_ref,
+    n_space, n_rep, per_piece, piece_rows, grad_scale,
+    share_ref, x_hbm, pre_hbm, cot_hbm, cw_hbm, ew_hbm,
     gi_hbm, gc_hbm, ge_hbm,
-    x_ref, cw_ref, weighted, hid_send, hid_recv, act_send, act_recv,
+    x_ref, pre_ref, cot_ref, cw_ref, ew_ref, weighted, hid_send, hid_recv, act_send, act_recv,
     spread, taps_in, grads, grads_next, below, gi_ref, mixed,
     acc, landing, total,
     load_sem, store_sem, hid_sems, act_sems, below_sems, rs_send, rs_recv, ag_send, ag_recv,
@@ -56,10 +58,11 @@
             return (s, at * n_core + here["core"])
         return (s, here["y"] * n_core + at)
 
-    load_x = pltpu.make_async_copy(x_hbm, x_ref, load_sem.at[0])
-    load_cw = pltpu.make_async_copy(cw_hbm, cw_ref, load_sem.at[1])
-    load_x.start()
-    load_cw.start()
+    pairs = ((cot_hbm, cot_ref), (ew_hbm, ew_ref), (pre_hbm, pre_ref), (x_hbm, x_ref), (cw_hbm, cw_ref))
+    loads = [pltpu.make_async_copy(a, b, load_sem.at[k]) for k, (a, b) in enumerate(pairs)]
+    load_cot, load_ew, load_pre, load_x, load_cw = loads
+    for load in loads:
+        load.start()
 
     barrier = pltpu.get_barrier_semaphore()
     partners = [((s + d) % n_space, r) for d in range(1, n_space)]
@@ -70,10 +73,13 @@
             barrier, inc=1, device_id=partner, device_id_type=pl.DeviceIdType.MESH
         )
 
+    load_cot.wait()
     weighted[...] = (cot_ref[...].astype(F32) * share_ref[0]).astype(BF16)
+    load_ew.wait()
     hidden = dot(weighted[...], ew_ref[...], 1, 1).astype(BF16)
     for j in range(n_space):
         hid_send[j] = hidden[j * block : (j + 1) * block]
+    load_pre.wait()
     for j in range(n_space):
         for i in range(half_rows):
             rows = pre_ref[i, j * band : (j + 1) * band, :].astype(F32)
@@ -99,7 +105,6 @@
         return copies
 
     hid_copies = exchange(hid_send, hid_recv, hid_sems)
-    act_copies = exchange(act_send, act_recv, act_sems)
 
     out_at = lax.broadcasted_iota(jnp.int32, (2 * width, 2 * width), 0)
     in_at = lax.broadcasted_iota(jnp.int32, (2 * width, 2 * width), 1)
@@ -142,27 +147,49 @@
     def _():
         below_copy.start()
 
-    starts = [sum(piece_rows[:k]) for k in range(len(piece_rows))]
+    act_copies = exchange(act_send, act_recv, act_sems)
     span = half_rows * width
-
-    def conv_piece(k, row_tap):
+    deep = weighted.shape[1]
+    n_units = len(UNITS) + deep // channels
+    n_pieces = -(-n_units // per_piece)
+
+    def unit_row(unit):
+        return unit // per_piece * piece_rows + unit % per_piece * channels
+
+    def conv_unit(unit):
+        row_tap, col_tap = UNITS[unit]
         first = width if row_tap == 0 else 0
-        for col_tap in range(3):
-            grad = grads_next if col_tap == 0 else grads
-            at = starts[k] + col_tap * channels
+        grad = grads_next if col_tap == 0 else grads
+        at = unit_row(unit)
+        acc[at : at + channels, :] = dot(
+            taps_in[(row_tap + 1) % 2, (col_tap + 1) % 2], grad[first : first + span, :], 1, 0
+        )
+
+    def expand_units():
+        for copy in act_copies:
+            copy.wait()
+        active = act_recv[...].astype(F32).reshape(n_space * block, channels).astype(BF16)
+        for k in range(deep // channels):
+            at = unit_row(len(UNITS) + k)
             acc[at : at + channels, :] = dot(
-                taps_in[(row_tap + 1) % 2, (col_tap + 1) % 2], grad[first : first + span, :], 1, 0
+                active, weighted[:, k * channels : (k + 1) * channels], 0, 0
             )
 
+    def low_units():
+        @pl.when(s < n_space - 1)
+        def _():
+            below_copy.wait_recv()
+
+        last = jnp.where(s < n_space - 1, 1.0, 0.0)
+        put_grad(half_rows, jnp.where(last > 0.5, below[...].astype(F32), 0.0))
+        for unit in range(6, 9):
+            conv_unit(unit)
+
     def piece(k):
-        if piece_rows[k] > valid_rows[k]:
-            acc[starts[k] + valid_rows[k] : starts[k] + piece_rows[k], :] = jnp.zeros(
-                (piece_rows[k] - valid_rows[k], acc.shape[1]), F32
-            )
-        base, length = starts[k], piece_rows[k]
-        slot, sem = starts[k], 0
+        base, length = k * piece_rows, piece_rows
+        slot, sem = base, 0
         levels = []
-        for axis in (LEAD,) + ORDERS[k] + ("z",):
+        for axis in ("core",) + tuple(ORDERS[k % len(ORDERS)]):
             n, at = sizes[axis], here[axis]
             if n == 1:
                 continue
@@ -184,7 +211,7 @@
                 slots.append(slot)
                 slot += sub
                 sem += 1
-            yield
+            yield axis, sub
             for copy in copies:
                 copy.wait()
             base = base + at * sub
@@ -195,7 +222,7 @@
             acc[own, :] = value
             length = sub
             levels.append((axis, n, at, base, sub))
-        total[own, :] = value
+        total[own, :] = value * grad_scale
         sem = 0
         for axis, n, at, base, sub in reversed(levels):
             copies = []
@@ -213,86 +240,104 @@
                 )
                 copies[-1].start()
                 sem += 1
-            yield
+            yield axis, sub
             for copy in copies:
                 copy.wait()
-
-    pieces = [piece(k) for k in range(4)]
-    conv_piece(0, 1)
-    next(pieces[0])
-    conv_piece(1, 2)
-    next(pieces[1])
-
-    @pl.when(s < n_space - 1)
-    def _():
-        below_copy.wait_recv()
-
-    last = jnp.where(s < n_space - 1, 1.0, 0.0)
-    lower = below[...].astype(F32)
-    put_grad(half_rows, jnp.where(last > 0.5, lower, 0.0))
-    next(pieces[0])
-    conv_piece(2, 0)
-    next(pieces[2])
-    next(pieces[1])
-    for copy in act_copies:
-        copy.wait()
-    active = act_recv[...].astype(F32).reshape(n_space * block, channels).astype(BF16)
-    deep = weighted.shape[1]
-    for k in range(deep // channels):
-        at = starts[3] + k * channels
-        acc[at : at + channels, :] = dot(
-            active, weighted[:, k * channels : (k + 1) * channels], 0, 0
-        )
-    next(pieces[3])
-    next(pieces[2])
-    next(pieces[3])
-
-    load_cw.wait()
+        for unit in range(k * per_piece, min((k + 1) * per_piece, n_units)):
+            rows = total.at[pl.ds(unit_row(unit), channels)]
+            if unit < len(UNITS):
+                p, q = UNITS[unit]
+                target = gc_hbm.at[p, pl.ds(q * channels, channels)]
+            else:
+                target = ge_hbm.at[:, pl.ds((unit - len(UNITS)) * channels, channels)]
+            stores.append(
+                pltpu.make_async_copy(rows, target, store_sem.at[2 * half_rows + unit])
+            )
+            stores[-1].start()
 
     def term(first, row_tap, col_tap):
         grad = grads_next if col_tap == 0 else grads
         return dot(grad[first : first + span, :], cw_ref[row_tap, col_tap], 1, 1)
 
+    def input_parts():
+        load_cw.wait()
+        for row_parity in range(2):
+            pairs = [(0, 1)] if row_parity == 0 else [(0, 2), (width, 0)]
+            for parity in range(2):
+                cols = (1,) if parity == 0 else (2, 0)
+                terms = [term(first, p, q) for first, p in pairs for q in cols]
+                mixed[parity] = functools.reduce(jnp.add, terms).astype(BF16)
+                yield
+            for i in range(half_rows):
+                both = jnp.concatenate(
+                    [mixed[parity, i * width : (i + 1) * width, :] for parity in range(2)], axis=0
+                )
+                row = 2 * i + row_parity
+                gi_ref[row] = dot(spread[...], both, 1, 0).astype(BF16)
+                stores.append(
+                    pltpu.make_async_copy(gi_ref.at[row], gi_hbm.at[row], store_sem.at[row])
+                )
+                stores[-1].start()
+                yield
+
     stores = []
-    for row_parity in range(2):
-        pairs = [(0, 1)] if row_parity == 0 else [(0, 2), (width, 0)]
-        for parity in range(2):
-            cols = (1,) if parity == 0 else (2, 0)
-            terms = [term(first, p, q) for first, p in pairs for q in cols]
-            mixed[parity] = functools.reduce(jnp.add, terms).astype(BF16)
-        for i in range(half_rows):
-            both = jnp.concatenate(
-                [mixed[parity, i * width : (i + 1) * width, :] for parity in range(2)], axis=0
-            )
-            row = 2 * i + row_parity
-            gi_ref[row] = dot(spread[...], both, 1, 0).astype(BF16)
-            stores.append(
-                pltpu.make_async_copy(gi_ref.at[row], gi_hbm.at[row], store_sem.at[row])
-            )
-            stores[-1].start()
-
-    slot = 2 * half_rows
-    waiting = list(range(4))
-    while waiting:
-        for k in list(waiting):
-            if next(pieces[k], "end") != "end":
-                continue
-            waiting.remove(k)
-            if k < 3:
-                rows = total.at[pl.ds(starts[k], valid_rows[k])]
-                outs = [(rows, gc_hbm.at[(1, 2, 0)[k]])]
-            else:
-                outs = [
-                    (
-                        total.at[pl.ds(starts[k] + m * channels, channels)],
-                        ge_hbm.at[:, pl.ds(m * channels, channels)],
+    pieces = [piece(k) for k in range(n_pieces)]
+    filler = input_parts()
+    line_free = dict.fromkeys(sizes, 0.0)
+    line_cost = {"core": 1 / 6, "x": 2.0, "y": 2.0, "z": 2.0 * (sizes["z"] // 2) ** 2}
+    per_row = channels * 4e-5
+    done_units = set()
+    begun = set()
+    events = []
+    clock = 0.0
+
+    def advance(k):
+        stage = next(pieces[k], None)
+        if stage is not None:
+            axis, sub = stage
+            begin = max(clock, line_free[axis])
+            line_free[axis] = begin + sub * per_row * line_cost[axis]
+            heapq.heappush(events, (line_free[axis] + 1.5, 2, k))
+
+    def ready(units):
+        done_units.update(units)
+        for k in range(n_pieces):
+            members = range(k * per_piece, min((k + 1) * per_piece, n_units))
+            if k not in begun and done_units.issuperset(members):
+                begun.add(k)
+                used = len(members) * channels
+                if used < piece_rows:
+                    acc[k * piece_rows + used : (k + 1) * piece_rows, :] = jnp.zeros(
+                        (piece_rows - used, channels), F32
                     )
-                    for m in range(deep // channels)
-                ]
-            for source, target in outs:
-                stores.append(pltpu.make_async_copy(source, target, store_sem.at[slot]))
-                stores[-1].start()
-                slot += 1
+                advance(k)
+
+    heapq.heappush(events, (4.0, 0, 0))
+    heapq.heappush(events, (7.0, 1, 0))
+    for unit in range(6):
+        conv_unit(unit)
+        ready([unit])
+        clock += 0.2
+    low_done = False
+    while events:
+        while low_done and events[0][0] > clock + 0.3 and next(filler, "end") != "end":
+            clock += 0.4
+        when, kind, k = heapq.heappop(events)
+        clock = max(clock, when)
+        if kind == 0:
+            low_units()
+            low_done = True
+            ready([6, 7, 8])
+            clock += 0.6
+        elif kind == 1:
+            expand_units()
+            ready(range(len(UNITS), n_units))
+            clock += 0.8
+        else:
+            advance(k)
+            clock += 0.1
+    for _ in filler:
+        pass
 
     @pl.when(s > 0)
     def _():
@@ -309,16 +354,18 @@
     _, deep_rows, band, deep = deep_cotangent.shape
     devices = n_space * n_rep
     block = half_rows * band
-    valid_rows = [3 * channels] * 3 + [deep]
-    piece_rows = [padded_rows(rows, devices) for rows in valid_rows]
-    all_rows = sum(piece_rows)
+    per_piece = -(-8 * devices // channels)
+    piece_rows = padded_rows(per_piece * channels, devices)
+    n_units = len(UNITS) + deep // channels
+    n_pieces = -(-n_units // per_piece)
+    all_rows = n_pieces * piece_rows
+    grad_scale = float(n_rep * half_rows * n_space * width) ** (-0.5)
     sizes = layout(n_space, n_rep)
     copies = sum(n - 1 for n in sizes.values())
-    vmem = pl.BlockSpec(memory_space=pltpu.VMEM)
     anywhere = pl.BlockSpec(memory_space=pl.ANY)
     dma = pltpu.SemaphoreType.DMA
     grad_input, conv_sum, expand_sum = pl.pallas_call(
-        functools.partial(kernel, n_space, n_rep, piece_rows, valid_rows),
+        functools.partial(kernel, n_space, n_rep, per_piece, piece_rows, grad_scale),
         out_shape=(
             jax.ShapeDtypeStruct((in_rows, cols, channels), BF16),
             jax.ShapeDtypeStruct((3, 3 * channels, channels), F32),
@@ -326,16 +373,15 @@
         ),
         in_specs=[
             pl.BlockSpec(memory_space=pltpu.SMEM),
-            anywhere,
-            vmem,
-            vmem,
-            anywhere,
-            vmem,
+            *[pl.BlockSpec(memory_space=pltpu.HBM)] * 5,
         ],
         out_specs=(anywhere, anywhere, anywhere),
         scratch_shapes=[
             pltpu.VMEM((in_rows, cols, channels), BF16),
+            pltpu.VMEM(stem_preact.shape[1:], BF16),
+            pltpu.VMEM((deep_rows * band, deep), BF16),
             pltpu.VMEM(conv_weight.shape, BF16),
+            pltpu.VMEM(expand_weight.shape, BF16),
             pltpu.VMEM((deep_rows * band, deep), BF16),
             pltpu.VMEM((n_space, block, channels), BF16),
             pltpu.VMEM((n_space, block, channels), BF16),
@@ -351,18 +397,18 @@
             pltpu.VMEM((all_rows, channels), F32),
             pltpu.VMEM((all_rows, channels), F32),
             pltpu.VMEM((all_rows, channels), F32),
-            dma((2,)),
-            dma((in_rows + 3 + deep // channels,)),
+            dma((5,)),
+            dma((in_rows + n_units,)),
             dma((2, n_space)),
             dma((2, n_space)),
             dma((2,)),
-            dma((4, copies)),
-            dma((4, copies)),
-            dma((4, copies)),
-            dma((4, copies)),
+            dma((n_pieces, copies)),
+            dma((n_pieces, copies)),
+            dma((n_pieces, copies)),
+            dma((n_pieces, copies)),
         ],
         compiler_params=pltpu.CompilerParams(
-            collective_id=0, has_side_effects=True, vmem_limit_bytes=56 * 1024 * 1024
+            collective_id=0, has_side_effects=True, vmem_limit_bytes=VMEM_LIMIT
         ),
     )(
         share,
@@ -372,9 +418,7 @@
         conv_weight,
         expand_weight,
     )
-    grad_scale = float(n_rep * half_rows * n_space * width) ** (-0.5)
-    grad_conv = conv_sum.reshape(3, 3, channels, channels) * grad_scale
-    return (grad_input[None], grad_conv, expand_sum * grad_scale)
+    return (grad_input[None], conv_sum.reshape(3, 3, channels, channels), expand_sum)
 
 
 def solution(mesh):

time: 79.7 us -> 74.2 us (0.931)
  the two profiles are of different devices: /device:TPU:25 before, /device:TPU:0 now
where the time goes in v2:
time: 74.2 us; the launch traced here: 73.9 us
  Pallas kernels  63.6 us (86%)
  local copies, waits for them, and re-layouts  9.05 us (12%)
  between operations  1.3 us (2%)
    pallas_call x1, Pallas kernels, body(): pl.pallas_call(functools.partial(kernel, n_space, n_rep, per_piece, piece...  63.6 us
    unnamed x13, local copies, waits for them, and re-layouts  9.05 us

profile of v2, /device:TPU:0, one launch (start us, length us, event | category | flops | bytes accessed | tf_op | source)
XLA Modules:
  0.0 73.9 jit_solution(741147318316430651)
XLA Ops:
  1.3 0.0 copy-start
  1.3 1.3 %copy-done = bf16[3,3,256,256]{3,2,1,0:T(8,128)(2,1)S(1)} copy-done((bf16[3,3,256,256]{3,2,1,0:T(8,128)(2,1)S(1)}, bf16[3,3,256,256]{3,2,1,0:T(8,128)(2,1)}, u32[]{:S(2)}) %copy-start) | copy-done | bytes 1179672
  2.6 0.0 copy-start.1
  2.6 1.2 %copy-done.1 = bf16[1,4,512,256]{3,2,1,0:T(8,128)(2,1)S(1)} copy-done((bf16[1,4,512,256]{3,2,1,0:T(8,128)(2,1)S(1)}, bf16[1,4,512,256]{3,2,1,0:T(8,128)(2,1)}, u32[]{:S(2)}) %copy-start.1) | copy-done | bytes 1048600
  3.8 0.0 copy-start.2
  3.8 1.2 %copy-done.2 = bf16[1,16,32,1024]{3,2,1,0:T(8,128)(2,1)S(1)} copy-done((bf16[1,16,32,1024]{3,2,1,0:T(8,128)(2,1)S(1)}, bf16[1,16,32,1024]{3,2,1,0:T(8,128)(2,1)}, u32[]{:S(2)}) %copy-start.2) | copy-done | bytes 1048600
  5.0 0.0 copy-start.3
  5.0 1.0 %copy-done.3 = bf16[256,1024]{1,0:T(8,128)(2,1)S(1)} copy-done((bf16[256,1024]{1,0:T(8,128)(2,1)S(1)}, bf16[256,1024]{1,0:T(8,128)(2,1)}, u32[]{:S(2)}) %copy-start.3) | copy-done | bytes 524312
  6.0 0.0 copy-start.4
  6.0 0.9 %copy-done.4 = bf16[1,2,256,256]{3,2,1,0:T(8,128)(2,1)S(1)} copy-done((bf16[1,2,256,256]{3,2,1,0:T(8,128)(2,1)S(1)}, bf16[1,2,256,256]{3,2,1,0:T(8,128)(2,1)}, u32[]{:S(2)}) %copy-start.4) | copy-done | bytes 262168
  7.0 63.6 %shard_map.85 = (bf16[4,512,256]{2,1,0:T(8,128)(2,1)S(1)}, f32[3,768,256]{2,1,0:T(8,128)S(1)}, f32[256,1024]{1,0:T(8,128)S(1)}) custom-call(f32[1]{0:T(128)S(6)} %div.3.share_ref, bf16[4,512,256]{2,1,0:T(8,128)(2,1)S(1)} %bitcast.7, bf16[2,256,256]{2,1,0:T(8,128)(2,1)S(1)} %bitcast.9, bf16[512,1024]{1,0:T(8,128)(2,1)S(1)} %bitcast.8, ...), custom_call_target="tpu_custom_call" | custom-call | tf_op jit(solution)/shard_map/pallas_call | solution.py:367
  70.6 1.0 %copy.13 = bf16[1,4,512,256]{3,2,1,0:T(8,128)(2,1)} copy(bf16[1,4,512,256]{3,2,1,0:T(8,128)(2,1)S(1)} %bitcast.6) | data formatting | bytes 2097152
  71.5 1.4 %copy.14 = f32[3,3,256,256]{3,2,1,0:T(8,128)} copy(f32[3,3,256,256]{3,2,1,0:T(8,128)S(1)} %bitcast.5) | data formatting | bytes 4718592
  73.0 1.0 %copy.15 = f32[256,1024]{1,0:T(8,128)} copy(f32[256,1024]{1,0:T(8,128)S(1)} %get-tuple-element.14) | data formatting | bytes 2097152
Async XLA Ops:
  1.3 1.3 %copy-start = (bf16[3,3,256,256]{3,2,1,0:T(8,128)(2,1)S(1)}, bf16[3,3,256,256]{3,2,1,0:T(8,128)(2,1)}, u32[]{:S(2)}) copy-start(bf16[3,3,256,256]{3,2,1,0:T(8,128)(2,1)} %cw_hbm.1) | copy-start | bytes 3538948
  2.6 1.2 %copy-start.1 = (bf16[1,4,512,256]{3,2,1,0:T(8,128)(2,1)S(1)}, bf16[1,4,512,256]{3,2,1,0:T(8,128)(2,1)}, u32[]{:S(2)}) copy-start(bf16[1,4,512,256]{3,2,1,0:T(8,128)(2,1)} %param.6) | copy-start | bytes 3145732
  3.8 1.2 %copy-start.2 = (bf16[1,16,32,1024]{3,2,1,0:T(8,128)(2,1)S(1)}, bf16[1,16,32,1024]{3,2,1,0:T(8,128)(2,1)}, u32[]{:S(2)}) copy-start(bf16[1,16,32,1024]{3,2,1,0:T(8,128)(2,1)} %param.8) | copy-start | bytes 3145732
  5.0 1.0 %copy-start.3 = (bf16[256,1024]{1,0:T(8,128)(2,1)S(1)}, bf16[256,1024]{1,0:T(8,128)(2,1)}, u32[]{:S(2)}) copy-start(bf16[256,1024]{1,0:T(8,128)(2,1)} %ew_hbm.1) | copy-start | bytes 1572868
  6.0 0.9 %copy-start.4 = (bf16[1,2,256,256]{3,2,1,0:T(8,128)(2,1)S(1)}, bf16[1,2,256,256]{3,2,1,0:T(8,128)(2,1)}, u32[]{:S(2)}) copy-start(bf16[1,2,256,256]{3,2,1,0:T(8,128)(2,1)} %param.7) | copy-start | bytes 786436

commit v3 on v2

--- a/solution.py
+++ b/solution.py
@@ -9,7 +9,7 @@
 from jax.sharding import PartitionSpec as P
 
 TILES = 64
-VMEM_LIMIT = 32 * 1024 * 1024
+VMEM_LIMIT = 56 * 1024 * 1024
 F32, BF16 = jnp.float32, jnp.bfloat16
 ORDERS = ("xyz", "yxz", "xzy", "yxz", "xyz", "yzx")
 UNITS = tuple((p, q) for p in (1, 2, 0) for q in range(3))
@@ -58,9 +58,9 @@
             return (s, at * n_core + here["core"])
         return (s, here["y"] * n_core + at)
 
-    pairs = ((cot_hbm, cot_ref), (ew_hbm, ew_ref), (pre_hbm, pre_ref), (x_hbm, x_ref), (cw_hbm, cw_ref))
+    pairs = ((pre_hbm, pre_ref), (cot_hbm, cot_ref), (ew_hbm, ew_ref), (x_hbm, x_ref), (cw_hbm, cw_ref))
     loads = [pltpu.make_async_copy(a, b, load_sem.at[k]) for k, (a, b) in enumerate(pairs)]
-    load_cot, load_ew, load_pre, load_x, load_cw = loads
+    load_pre, load_cot, load_ew, load_x, load_cw = loads
     for load in loads:
         load.start()
 
@@ -73,17 +73,14 @@
             barrier, inc=1, device_id=partner, device_id_type=pl.DeviceIdType.MESH
         )
 
-    load_cot.wait()
-    weighted[...] = (cot_ref[...].astype(F32) * share_ref[0]).astype(BF16)
-    load_ew.wait()
-    hidden = dot(weighted[...], ew_ref[...], 1, 1).astype(BF16)
-    for j in range(n_space):
-        hid_send[j] = hidden[j * block : (j + 1) * block]
     load_pre.wait()
     for j in range(n_space):
         for i in range(half_rows):
             rows = pre_ref[i, j * band : (j + 1) * band, :].astype(F32)
             act_send[j, i * band : (i + 1) * band, :] = jnp.maximum(rows, 0.0).astype(BF16)
+    load_cot.wait()
+    weighted[...] = (cot_ref[...].astype(F32) * share_ref[0]).astype(BF16)
+    load_ew.wait()
     pl.semaphore_wait(barrier, len(partners))
 
     def exchange(source, target, sems):
@@ -104,6 +101,10 @@
         target[s] = source[s]
         return copies
 
+    act_copies = exchange(act_send, act_recv, act_sems)
+    hidden = dot(weighted[...], ew_ref[...], 1, 1).astype(BF16)
+    for j in range(n_space):
+        hid_send[j] = hidden[j * block : (j + 1) * block]
     hid_copies = exchange(hid_send, hid_recv, hid_sems)
 
     out_at = lax.broadcasted_iota(jnp.int32, (2 * width, 2 * width), 0)
@@ -119,35 +120,6 @@
                 :, parity * width : (parity + 1) * width
             ]
 
-    for copy in hid_copies:
-        copy.wait()
-
-    column = lax.broadcasted_iota(jnp.int32, (width, channels), 0)
-
-    def put_grad(i, value):
-        grads[i * width : (i + 1) * width, :] = value.astype(BF16)
-        moved = jnp.where(column < width - 1, pltpu.roll(value, width - 1, 0), 0.0)
-        grads_next[i * width : (i + 1) * width, :] = moved.astype(BF16)
-
-    for i in range(half_rows):
-        arrived = jnp.concatenate(
-            [hid_recv[j, i * band : (i + 1) * band, :].astype(F32) for j in range(n_space)], axis=0
-        )
-        put_grad(i, jnp.where(pre_ref[i].astype(F32) > 0, arrived, 0.0))
-    below_copy = pltpu.make_async_remote_copy(
-        src_ref=grads.at[0:width],
-        dst_ref=below,
-        send_sem=below_sems.at[0],
-        recv_sem=below_sems.at[1],
-        device_id=((s + n_space - 1) % n_space, r),
-        device_id_type=pl.DeviceIdType.MESH,
-    )
-
-    @pl.when(s > 0)
-    def _():
-        below_copy.start()
-
-    act_copies = exchange(act_send, act_recv, act_sems)
     span = half_rows * width
     deep = weighted.shape[1]
     n_units = len(UNITS) + deep // channels
@@ -312,12 +284,47 @@
                     )
                 advance(k)
 
-    heapq.heappush(events, (4.0, 0, 0))
-    heapq.heappush(events, (7.0, 1, 0))
+    column = lax.broadcasted_iota(jnp.int32, (width, channels), 0)
+
+    def put_grad(i, value):
+        grads[i * width : (i + 1) * width, :] = value.astype(BF16)
+        moved = jnp.where(column < width - 1, pltpu.roll(value, width - 1, 0), 0.0)
+        grads_next[i * width : (i + 1) * width, :] = moved.astype(BF16)
+
+    expand_units()
+    ready(range(len(UNITS), n_units))
+    while events and events[0][0] < 3.0:
+        clock, _, k = heapq.heappop(events)
+        advance(k)
+    for copy in hid_copies:
+        copy.wait()
+
+    for i in range(half_rows):
+        arrived = jnp.concatenate(
+            [hid_recv[j, i * band : (i + 1) * band, :].astype(F32) for j in range(n_space)], axis=0
+        )
+        put_grad(i, jnp.where(pre_ref[i].astype(F32) > 0, arrived, 0.0))
+    below_copy = pltpu.make_async_remote_copy(
+        src_ref=grads.at[0:width],
+        dst_ref=below,
+        send_sem=below_sems.at[0],
+        recv_sem=below_sems.at[1],
+        device_id=((s + n_space - 1) % n_space, r),
+        device_id_type=pl.DeviceIdType.MESH,
+    )
+
+    @pl.when(s > 0)
+    def _():
+        below_copy.start()
+
+    clock = 4.0
     for unit in range(6):
         conv_unit(unit)
         ready([unit])
         clock += 0.2
+        while events and events[0][0] < clock:
+            advance(heapq.heappop(events)[2])
+    heapq.heappush(events, (8.0, 0, 0))
     low_done = False
     while events:
         while low_done and events[0][0] > clock + 0.3 and next(filler, "end") != "end":
@@ -329,10 +336,6 @@
             low_done = True
             ready([6, 7, 8])
             clock += 0.6
-        elif kind == 1:
-            expand_units()
-            ready(range(len(UNITS), n_units))
-            clock += 0.8
         else:
             advance(k)
             clock += 0.1

time: 74.2 us -> 79.6 us (1.073)
  Pallas kernels: 63.6 us -> 71.6 us
  local copies, waits for them, and re-layouts: 9.05 us -> 6.55 us
    pallas_call x1, Pallas kernels: 63.6 us -> 71.6 us  [body(): pl.pallas_call(functools.partial(kernel, n_space, n_rep, per_piece, piece...]
    unnamed x13 -> x5, local copies, waits for them, and re-layouts: 9.05 us -> 6.55 us
where the time goes in v3:
time: 79.6 us; the launch traced here: 79.5 us
  Pallas kernels  71.6 us (90%)
  local copies, waits for them, and re-layouts  6.55 us (8%)
  between operations  1.29 us (2%)
    pallas_call x1, Pallas kernels, body(): pl.pallas_call(functools.partial(kernel, n_space, n_rep, per_piece, piece...  71.6 us
    unnamed x5, local copies, waits for them, and re-layouts  6.55 us

profile of v3, /device:TPU:0, one launch (start us, length us, event | category | flops | bytes accessed | tf_op | source)
XLA Modules:
  0.0 79.5 jit_solution(6303966853654099869)
XLA Ops:
  1.3 71.6 %shard_map.85 = (bf16[4,512,256]{2,1,0:T(8,128)(2,1)}, f32[3,768,256]{2,1,0:T(8,128)}, f32[256,1024]{1,0:T(8,128)}) custom-call(f32[1]{0:T(128)S(6)} %div.3.share_ref, bf16[4,512,256]{2,1,0:T(8,128)(2,1)} %bitcast.7, bf16[2,256,256]{2,1,0:T(8,128)(2,1)} %bitcast.9, bf16[512,1024]{1,0:T(8,128)(2,1)} %bitcast.8, bf16[3,3,256,256]{3,2,1,0:T(8,128)(2,1)} %cw_hbm.1, ...), custom_call_target="tpu_custom_call" | custom-call | tf_op jit(solution)/shard_map/pallas_call | solution.py:370
  72.9 2.3 %copy.13 = bf16[1,4,512,256]{3,2,1,0:T(8,128)(2,1)} copy(bf16[1,4,512,256]{3,2,1,0:T(8,128)(2,1)} %bitcast.6) | data formatting | bytes 2097152
  75.2 0.0 copy-start
  75.2 3.3 %copy.14 = f32[3,3,256,256]{3,2,1,0:T(8,128)} copy(f32[3,3,256,256]{3,2,1,0:T(8,128)} %bitcast.5) | data formatting | bytes 4718592
  78.5 0.0 copy-done
  78.5 1.0 %copy.15 = f32[256,1024]{1,0:T(8,128)} copy(f32[256,1024]{1,0:T(8,128)S(1)} %copy-done) | data formatting | bytes 2097152
Async XLA Ops:
  75.2 3.3 %copy-start = (f32[256,1024]{1,0:T(8,128)S(1)}, f32[256,1024]{1,0:T(8,128)}, u32[]{:S(2)}) copy-start(f32[256,1024]{1,0:T(8,128)} %get-tuple-element.14) | copy-start | bytes 3145732

commit v4 on v2

--- a/solution.py
+++ b/solution.py
@@ -11,7 +11,7 @@
 TILES = 64
 VMEM_LIMIT = 32 * 1024 * 1024
 F32, BF16 = jnp.float32, jnp.bfloat16
-ORDERS = ("xyz", "yxz", "xzy", "yxz", "xyz", "yzx")
+ORDERS = ("xyz", "yxz", "xzy", "yzx", "xyz", "yxz", "xyz")
 UNITS = tuple((p, q) for p in (1, 2, 0) for q in range(3))
 
 
@@ -156,6 +156,10 @@
     def unit_row(unit):
         return unit // per_piece * piece_rows + unit % per_piece * channels
 
+    def piece_length(k):
+        members = min((k + 1) * per_piece, n_units) - k * per_piece
+        return padded_rows(members * channels, n_space * n_rep)
+
     def conv_unit(unit):
         row_tap, col_tap = UNITS[unit]
         first = width if row_tap == 0 else 0
@@ -186,7 +190,7 @@
             conv_unit(unit)
 
     def piece(k):
-        base, length = k * piece_rows, piece_rows
+        base, length = k * piece_rows, piece_length(k)
         slot, sem = base, 0
         levels = []
         for axis in ("core",) + tuple(ORDERS[k % len(ORDERS)]):
@@ -306,9 +310,9 @@
             if k not in begun and done_units.issuperset(members):
                 begun.add(k)
                 used = len(members) * channels
-                if used < piece_rows:
-                    acc[k * piece_rows + used : (k + 1) * piece_rows, :] = jnp.zeros(
-                        (piece_rows - used, channels), F32
+                if used < piece_length(k):
+                    acc[k * piece_rows + used : k * piece_rows + piece_length(k), :] = jnp.zeros(
+                        (piece_length(k) - used, channels), F32
                     )
                 advance(k)
 
@@ -354,7 +358,7 @@
     _, deep_rows, band, deep = deep_cotangent.shape
     devices = n_space * n_rep
     block = half_rows * band
-    per_piece = -(-8 * devices // channels)
+    per_piece = max(2, -(-8 * devices // channels))
     piece_rows = padded_rows(per_piece * channels, devices)
     n_units = len(UNITS) + deep // channels
     n_pieces = -(-n_units // per_piece)

time: 74.2 us -> 79.2 us (1.067)
  Pallas kernels: 63.6 us -> 68.5 us
    pallas_call x1, Pallas kernels: 63.6 us -> 68.5 us  [body(): pl.pallas_call(functools.partial(kernel, n_space, n_rep, per_piece, piece...]
where the time goes in v4:
time: 79.2 us; the launch traced here: 78.8 us
  Pallas kernels  68.5 us (86%)
  local copies, waits for them, and re-layouts  9.05 us (11%)
  between operations  1.3 us (2%)
    pallas_call x1, Pallas kernels, body(): pl.pallas_call(functools.partial(kernel, n_space, n_rep, per_piece, piece...  68.5 us
    unnamed x13, local copies, waits for them, and re-layouts  9.05 us

profile of v4, /device:TPU:0, one launch (start us, length us, event | category | flops | bytes accessed | tf_op | source)
XLA Modules:
  0.0 78.8 jit_solution(5116274331509535658)
XLA Ops:
  1.3 0.0 copy-start
  1.3 1.3 %copy-done = bf16[3,3,256,256]{3,2,1,0:T(8,128)(2,1)S(1)} copy-done((bf16[3,3,256,256]{3,2,1,0:T(8,128)(2,1)S(1)}, bf16[3,3,256,256]{3,2,1,0:T(8,128)(2,1)}, u32[]{:S(2)}) %copy-start) | copy-done | bytes 1179672
  2.6 0.0 copy-start.1
  2.6 1.2 %copy-done.1 = bf16[1,4,512,256]{3,2,1,0:T(8,128)(2,1)S(1)} copy-done((bf16[1,4,512,256]{3,2,1,0:T(8,128)(2,1)S(1)}, bf16[1,4,512,256]{3,2,1,0:T(8,128)(2,1)}, u32[]{:S(2)}) %copy-start.1) | copy-done | bytes 1048600
  3.8 0.0 copy-start.2
  3.8 1.2 %copy-done.2 = bf16[1,16,32,1024]{3,2,1,0:T(8,128)(2,1)S(1)} copy-done((bf16[1,16,32,1024]{3,2,1,0:T(8,128)(2,1)S(1)}, bf16[1,16,32,1024]{3,2,1,0:T(8,128)(2,1)}, u32[]{:S(2)}) %copy-start.2) | copy-done | bytes 1048600
  5.0 0.0 copy-start.3
  5.0 1.0 %copy-done.3 = bf16[256,1024]{1,0:T(8,128)(2,1)S(1)} copy-done((bf16[256,1024]{1,0:T(8,128)(2,1)S(1)}, bf16[256,1024]{1,0:T(8,128)(2,1)}, u32[]{:S(2)}) %copy-start.3) | copy-done | bytes 524312
  6.0 0.0 copy-start.4
  6.0 0.9 %copy-done.4 = bf16[1,2,256,256]{3,2,1,0:T(8,128)(2,1)S(1)} copy-done((bf16[1,2,256,256]{3,2,1,0:T(8,128)(2,1)S(1)}, bf16[1,2,256,256]{3,2,1,0:T(8,128)(2,1)}, u32[]{:S(2)}) %copy-start.4) | copy-done | bytes 262168
  7.0 68.5 %shard_map.85 = (bf16[4,512,256]{2,1,0:T(8,128)(2,1)S(1)}, f32[3,768,256]{2,1,0:T(8,128)S(1)}, f32[256,1024]{1,0:T(8,128)S(1)}) custom-call(f32[1]{0:T(128)S(6)} %div.3.share_ref, bf16[4,512,256]{2,1,0:T(8,128)(2,1)S(1)} %bitcast.7, bf16[2,256,256]{2,1,0:T(8,128)(2,1)S(1)} %bitcast.9, bf16[512,1024]{1,0:T(8,128)(2,1)S(1)} %bitcast.8, ...), custom_call_target="tpu_custom_call" | custom-call | tf_op jit(solution)/shard_map/pallas_call | solution.py:371
  75.5 1.0 %copy.13 = bf16[1,4,512,256]{3,2,1,0:T(8,128)(2,1)} copy(bf16[1,4,512,256]{3,2,1,0:T(8,128)(2,1)S(1)} %bitcast.6) | data formatting | bytes 2097152
  76.5 1.4 %copy.14 = f32[3,3,256,256]{3,2,1,0:T(8,128)} copy(f32[3,3,256,256]{3,2,1,0:T(8,128)S(1)} %bitcast.5) | data formatting | bytes 4718592
  77.9 1.0 %copy.15 = f32[256,1024]{1,0:T(8,128)} copy(f32[256,1024]{1,0:T(8,128)S(1)} %get-tuple-element.14) | data formatting | bytes 2097152
Async XLA Ops:
  1.3 1.3 %copy-start = (bf16[3,3,256,256]{3,2,1,0:T(8,128)(2,1)S(1)}, bf16[3,3,256,256]{3,2,1,0:T(8,128)(2,1)}, u32[]{:S(2)}) copy-start(bf16[3,3,256,256]{3,2,1,0:T(8,128)(2,1)} %cw_hbm.1) | copy-start | bytes 3538948
  2.6 1.2 %copy-start.1 = (bf16[1,4,512,256]{3,2,1,0:T(8,128)(2,1)S(1)}, bf16[1,4,512,256]{3,2,1,0:T(8,128)(2,1)}, u32[]{:S(2)}) copy-start(bf16[1,4,512,256]{3,2,1,0:T(8,128)(2,1)} %param.6) | copy-start | bytes 3145732
  3.8 1.2 %copy-start.2 = (bf16[1,16,32,1024]{3,2,1,0:T(8,128)(2,1)S(1)}, bf16[1,16,32,1024]{3,2,1,0:T(8,128)(2,1)}, u32[]{:S(2)}) copy-start(bf16[1,16,32,1024]{3,2,1,0:T(8,128)(2,1)} %param.8) | copy-start | bytes 3145732
  5.0 1.0 %copy-start.3 = (bf16[256,1024]{1,0:T(8,128)(2,1)S(1)}, bf16[256,1024]{1,0:T(8,128)(2,1)}, u32[]{:S(2)}) copy-start(bf16[256,1024]{1,0:T(8,128)(2,1)} %ew_hbm.1) | copy-start | bytes 1572868
  6.0 0.9 %copy-start.4 = (bf16[1,2,256,256]{3,2,1,0:T(8,128)(2,1)S(1)}, bf16[1,2,256,256]{3,2,1,0:T(8,128)(2,1)}, u32[]{:S(2)}) copy-start(bf16[1,2,256,256]{3,2,1,0:T(8,128)(2,1)} %param.7) | copy-start | bytes 786436

commit v5 on v2

--- a/solution.py
+++ b/solution.py
@@ -11,7 +11,7 @@
 TILES = 64
 VMEM_LIMIT = 32 * 1024 * 1024
 F32, BF16 = jnp.float32, jnp.bfloat16
-ORDERS = ("xyz", "yxz", "xzy", "yxz", "xyz", "yzx")
+ORDERS = ("yxz", "xyz", "xyz", "yxz", "yxz", "zyx", "zxy", "yxz", "yxz", "yxz", "xyz", "xyz", "xyz")
 UNITS = tuple((p, q) for p in (1, 2, 0) for q in range(3))
 
 

time: 74.2 us -> 70.7 us (0.953)
  Pallas kernels: 63.6 us -> 60 us
    pallas_call x1, Pallas kernels: 63.6 us -> 60 us  [body(): pl.pallas_call(functools.partial(kernel, n_space, n_rep, per_piece, piece...]
where the time goes in v5:
time: 70.7 us; the launch traced here: 70.4 us
  Pallas kernels  60 us (85%)
  local copies, waits for them, and re-layouts  9.05 us (13%)
  between operations  1.3 us (2%)
    pallas_call x1, Pallas kernels, body(): pl.pallas_call(functools.partial(kernel, n_space, n_rep, per_piece, piece...  60 us
    unnamed x13, local copies, waits for them, and re-layouts  9.05 us

profile of v5, /device:TPU:0, one launch (start us, length us, event | category | flops | bytes accessed | tf_op | source)
XLA Modules:
  0.0 70.4 jit_solution(16827701263994736233)
XLA Ops:
  1.3 0.0 copy-start
  1.3 1.3 %copy-done = bf16[3,3,256,256]{3,2,1,0:T(8,128)(2,1)S(1)} copy-done((bf16[3,3,256,256]{3,2,1,0:T(8,128)(2,1)S(1)}, bf16[3,3,256,256]{3,2,1,0:T(8,128)(2,1)}, u32[]{:S(2)}) %copy-start) | copy-done | bytes 1179672
  2.6 0.0 copy-start.1
  2.6 1.2 %copy-done.1 = bf16[1,4,512,256]{3,2,1,0:T(8,128)(2,1)S(1)} copy-done((bf16[1,4,512,256]{3,2,1,0:T(8,128)(2,1)S(1)}, bf16[1,4,512,256]{3,2,1,0:T(8,128)(2,1)}, u32[]{:S(2)}) %copy-start.1) | copy-done | bytes 1048600
  3.8 0.0 copy-start.2
  3.8 1.2 %copy-done.2 = bf16[1,16,32,1024]{3,2,1,0:T(8,128)(2,1)S(1)} copy-done((bf16[1,16,32,1024]{3,2,1,0:T(8,128)(2,1)S(1)}, bf16[1,16,32,1024]{3,2,1,0:T(8,128)(2,1)}, u32[]{:S(2)}) %copy-start.2) | copy-done | bytes 1048600
  5.0 0.0 copy-start.3
  5.0 1.0 %copy-done.3 = bf16[256,1024]{1,0:T(8,128)(2,1)S(1)} copy-done((bf16[256,1024]{1,0:T(8,128)(2,1)S(1)}, bf16[256,1024]{1,0:T(8,128)(2,1)}, u32[]{:S(2)}) %copy-start.3) | copy-done | bytes 524312
  6.0 0.0 copy-start.4
  6.0 0.9 %copy-done.4 = bf16[1,2,256,256]{3,2,1,0:T(8,128)(2,1)S(1)} copy-done((bf16[1,2,256,256]{3,2,1,0:T(8,128)(2,1)S(1)}, bf16[1,2,256,256]{3,2,1,0:T(8,128)(2,1)}, u32[]{:S(2)}) %copy-start.4) | copy-done | bytes 262168
  7.0 60.0 %shard_map.85 = (bf16[4,512,256]{2,1,0:T(8,128)(2,1)S(1)}, f32[3,768,256]{2,1,0:T(8,128)S(1)}, f32[256,1024]{1,0:T(8,128)S(1)}) custom-call(f32[1]{0:T(128)S(6)} %div.3.share_ref, bf16[4,512,256]{2,1,0:T(8,128)(2,1)S(1)} %bitcast.7, bf16[2,256,256]{2,1,0:T(8,128)(2,1)S(1)} %bitcast.9, bf16[512,1024]{1,0:T(8,128)(2,1)S(1)} %bitcast.8, ...), custom_call_target="tpu_custom_call" | custom-call | tf_op jit(solution)/shard_map/pallas_call | solution.py:367
  67.0 1.0 %copy.13 = bf16[1,4,512,256]{3,2,1,0:T(8,128)(2,1)} copy(bf16[1,4,512,256]{3,2,1,0:T(8,128)(2,1)S(1)} %bitcast.6) | data formatting | bytes 2097152
  68.0 1.4 %copy.14 = f32[3,3,256,256]{3,2,1,0:T(8,128)} copy(f32[3,3,256,256]{3,2,1,0:T(8,128)S(1)} %bitcast.5) | data formatting | bytes 4718592
  69.4 1.0 %copy.15 = f32[256,1024]{1,0:T(8,128)} copy(f32[256,1024]{1,0:T(8,128)S(1)} %get-tuple-element.14) | data formatting | bytes 2097152
Async XLA Ops:
  1.3 1.3 %copy-start = (bf16[3,3,256,256]{3,2,1,0:T(8,128)(2,1)S(1)}, bf16[3,3,256,256]{3,2,1,0:T(8,128)(2,1)}, u32[]{:S(2)}) copy-start(bf16[3,3,256,256]{3,2,1,0:T(8,128)(2,1)} %cw_hbm.1) | copy-start | bytes 3538948
  2.6 1.2 %copy-start.1 = (bf16[1,4,512,256]{3,2,1,0:T(8,128)(2,1)S(1)}, bf16[1,4,512,256]{3,2,1,0:T(8,128)(2,1)}, u32[]{:S(2)}) copy-start(bf16[1,4,512,256]{3,2,1,0:T(8,128)(2,1)} %param.6) | copy-start | bytes 3145732
  3.8 1.2 %copy-start.2 = (bf16[1,16,32,1024]{3,2,1,0:T(8,128)(2,1)S(1)}, bf16[1,16,32,1024]{3,2,1,0:T(8,128)(2,1)}, u32[]{:S(2)}) copy-start(bf16[1,16,32,1024]{3,2,1,0:T(8,128)(2,1)} %param.8) | copy-start | bytes 3145732
  5.0 1.0 %copy-start.3 = (bf16[256,1024]{1,0:T(8,128)(2,1)S(1)}, bf16[256,1024]{1,0:T(8,128)(2,1)}, u32[]{:S(2)}) copy-start(bf16[256,1024]{1,0:T(8,128)(2,1)} %ew_hbm.1) | copy-start | bytes 1572868
  6.0 0.9 %copy-start.4 = (bf16[1,2,256,256]{3,2,1,0:T(8,128)(2,1)S(1)}, bf16[1,2,256,256]{3,2,1,0:T(8,128)(2,1)}, u32[]{:S(2)}) copy-start(bf16[1,2,256,256]{3,2,1,0:T(8,128)(2,1)} %param.7) | copy-start | bytes 786436

commit v6 on v5

--- a/solution.py
+++ b/solution.py
@@ -34,9 +34,9 @@
 
 def kernel(
     n_space, n_rep, per_piece, piece_rows, grad_scale,
-    share_ref, x_hbm, pre_hbm, cot_hbm, cw_hbm, ew_hbm,
+    x_hbm, pre_hbm, cot_hbm, cw_hbm, ew_hbm,
     gi_hbm, gc_hbm, ge_hbm,
-    x_ref, pre_ref, cot_ref, cw_ref, ew_ref, weighted, hid_send, hid_recv, act_send, act_recv,
+    x_ref, pre_ref, cw_ref, ew_ref, weighted, hid_send, hid_recv, act_send, act_recv,
     spread, taps_in, grads, grads_next, below, gi_ref, mixed,
     acc, landing, total,
     load_sem, store_sem, hid_sems, act_sems, below_sems, rs_send, rs_recv, ag_send, ag_recv,
@@ -58,7 +58,7 @@
             return (s, at * n_core + here["core"])
         return (s, here["y"] * n_core + at)
 
-    pairs = ((cot_hbm, cot_ref), (ew_hbm, ew_ref), (pre_hbm, pre_ref), (x_hbm, x_ref), (cw_hbm, cw_ref))
+    pairs = ((cot_hbm, weighted), (ew_hbm, ew_ref), (pre_hbm, pre_ref), (x_hbm, x_ref), (cw_hbm, cw_ref))
     loads = [pltpu.make_async_copy(a, b, load_sem.at[k]) for k, (a, b) in enumerate(pairs)]
     load_cot, load_ew, load_pre, load_x, load_cw = loads
     for load in loads:
@@ -74,7 +74,6 @@
         )
 
     load_cot.wait()
-    weighted[...] = (cot_ref[...].astype(F32) * share_ref[0]).astype(BF16)
     load_ew.wait()
     hidden = dot(weighted[...], ew_ref[...], 1, 1).astype(BF16)
     for j in range(n_space):
@@ -349,6 +348,7 @@
 
 def body(n_space, n_rep, stem_input, stem_preact, deep_cotangent, tissue_tiles, conv_weight, expand_weight):
     share = tissue_tiles.astype(F32) / TILES
+    weighted = (deep_cotangent.astype(F32) * share[:, None, None, None]).astype(BF16)
     _, in_rows, cols, channels = stem_input.shape
     _, half_rows, width, _ = stem_preact.shape
     _, deep_rows, band, deep = deep_cotangent.shape
@@ -372,14 +372,12 @@
             jax.ShapeDtypeStruct((channels, deep), F32),
         ),
         in_specs=[
-            pl.BlockSpec(memory_space=pltpu.SMEM),
             *[pl.BlockSpec(memory_space=pltpu.HBM)] * 5,
         ],
         out_specs=(anywhere, anywhere, anywhere),
         scratch_shapes=[
             pltpu.VMEM((in_rows, cols, channels), BF16),
             pltpu.VMEM(stem_preact.shape[1:], BF16),
-            pltpu.VMEM((deep_rows * band, deep), BF16),
             pltpu.VMEM(conv_weight.shape, BF16),
             pltpu.VMEM(expand_weight.shape, BF16),
             pltpu.VMEM((deep_rows * band, deep), BF16),
@@ -411,10 +409,9 @@
             collective_id=0, has_side_effects=True, vmem_limit_bytes=VMEM_LIMIT
         ),
     )(
-        share,
         stem_input[0],
         stem_preact[0],
-        deep_cotangent.reshape(deep_rows * band, deep),
+        weighted.reshape(deep_rows * band, deep),
         conv_weight,
         expand_weight,
     )

time: 70.7 us -> 67.7 us (0.958)
  local copies, waits for them, and re-layouts: 9.05 us -> 4.58 us
  other arithmetic: 0 us -> 1.44 us
    unnamed x13 -> x11, local copies, waits for them, and re-layouts: 9.05 us -> 4.58 us
    convert_element_type x0 -> x1, other arithmetic: none -> 1.44 us  [body(): (deep_cotangent.astype(F32) * share[:, None, None, None]).astype(BF16)]
where the time goes in v6:
time: 67.7 us; the launch traced here: 67.5 us
  Pallas kernels  60 us (89%)
  local copies, waits for them, and re-layouts  4.58 us (7%)
  between operations  1.49 us (2%)
  other arithmetic  1.44 us (2%)
    pallas_call x1, Pallas kernels, body(): pl.pallas_call(functools.partial(kernel, n_space, n_rep, per_piece, piece...  60 us
    unnamed x11, local copies, waits for them, and re-layouts  4.58 us
    convert_element_type x1, other arithmetic, body(): (deep_cotangent.astype(F32) * share[:, None, None, None]).astype(BF16)  1.44 us

profile of v6, /device:TPU:0, one launch (start us, length us, event | category | flops | bytes accessed | tf_op | source)
XLA Modules:
  0.0 67.5 jit_solution(9542397815946252690)
XLA Ops:
  0.6 0.0 copy-start.2
  0.6 0.0 copy-start
  0.7 0.0 copy-start.3
  1.4 1.4 %multiply_convert_fusion = bf16[1,16,32,1024]{3,2,1,0:T(8,128)(2,1)S(1)} fusion(bf16[1,16,32,1024]{3,2,1,0:T(8,128)(2,1)} %param.8, f32[]{:T(128)} %bitcast.2), kind=kLoop, calls=%fused_computation | loop fusion | flops 1572864 | bytes 2097156 | tf_op jit(solution)/shard_map/convert_element_type | solution.py:351
  2.9 0.0 copy-done.2
  2.9 0.0 copy-done
  2.9 0.0 copy-done.3
  2.9 0.0 copy-start.1
  2.9 1.2 %copy-done.1 = bf16[1,4,512,256]{3,2,1,0:T(8,128)(2,1)S(1)} copy-done((bf16[1,4,512,256]{3,2,1,0:T(8,128)(2,1)S(1)}, bf16[1,4,512,256]{3,2,1,0:T(8,128)(2,1)}, u32[]{:S(2)}) %copy-start.1) | copy-done | bytes 1048600
  4.2 60.0 %shard_map.85 = (bf16[4,512,256]{2,1,0:T(8,128)(2,1)S(1)}, f32[3,768,256]{2,1,0:T(8,128)S(1)}, f32[256,1024]{1,0:T(8,128)S(1)}) custom-call(bf16[4,512,256]{2,1,0:T(8,128)(2,1)S(1)} %bitcast.9, bf16[2,256,256]{2,1,0:T(8,128)(2,1)S(1)} %bitcast.10, bf16[512,1024]{1,0:T(8,128)(2,1)S(1)} %bitcast.6, bf16[3,3,256,256]{3,2,1,0:T(8,128)(2,1)S(1)} %copy-done, ...), custom_call_target="tpu_custom_call" | custom-call | tf_op jit(solution)/shard_map/pallas_call | solution.py:367
  64.2 1.0 %copy.13 = bf16[1,4,512,256]{3,2,1,0:T(8,128)(2,1)} copy(bf16[1,4,512,256]{3,2,1,0:T(8,128)(2,1)S(1)} %bitcast.8) | data formatting | bytes 2097152
  65.1 1.4 %copy.14 = f32[3,3,256,256]{3,2,1,0:T(8,128)} copy(f32[3,3,256,256]{3,2,1,0:T(8,128)S(1)} %bitcast.7) | data formatting | bytes 4718592
  66.6 1.0 %copy.15 = f32[256,1024]{1,0:T(8,128)} copy(f32[256,1024]{1,0:T(8,128)S(1)} %get-tuple-element.14) | data formatting | bytes 2097152
Async XLA Ops:
  0.6 2.3 %copy-start.2 = (bf16[256,1024]{1,0:T(8,128)(2,1)S(1)}, bf16[256,1024]{1,0:T(8,128)(2,1)}, u32[]{:S(2)}) copy-start(bf16[256,1024]{1,0:T(8,128)(2,1)} %ew_hbm.1) | copy-start | bytes 1572868
  0.6 2.3 %copy-start = (bf16[3,3,256,256]{3,2,1,0:T(8,128)(2,1)S(1)}, bf16[3,3,256,256]{3,2,1,0:T(8,128)(2,1)}, u32[]{:S(2)}) copy-start(bf16[3,3,256,256]{3,2,1,0:T(8,128)(2,1)} %cw_hbm.1) | copy-start | bytes 3538948
  0.7 2.3 %copy-start.3 = (bf16[1,2,256,256]{3,2,1,0:T(8,128)(2,1)S(1)}, bf16[1,2,256,256]{3,2,1,0:T(8,128)(2,1)}, u32[]{:S(2)}) copy-start(bf16[1,2,256,256]{3,2,1,0:T(8,128)(2,1)} %param.7) | copy-start | bytes 786436
  2.9 1.2 %copy-start.1 = (bf16[1,4,512,256]{3,2,1,0:T(8,128)(2,1)S(1)}, bf16[1,4,512,256]{3,2,1,0:T(8,128)(2,1)}, u32[]{:S(2)}) copy-start(bf16[1,4,512,256]{3,2,1,0:T(8,128)(2,1)} %param.6) | copy-start | bytes 3145732
